TPU v7x, 32 devices: a whole 2x2x4 slice. The times are simulated.
32 devices in a mesh: parts: 2 (over y), group: 4 (over z), local: 4 (over x, core).
Axes of the slice: x: 2, y: 2, z: 4, core: 2. Of those that a mesh axis runs over, the one named last changes fastest.
Arguments:
- tokens: bfloat16 [4096, 3584], P(('parts', 'group', 'local')), parts along dimension 0, may hold values from -6 to 6
- routes: int32 [4096, 8], P(('parts', 'group', 'local')), parts along dimension 0, may hold values from 0 to 15, as said below
- gate_weights: bfloat16 [4096, 8], P(('parts', 'group', 'local')), parts along dimension 0, may hold values from 0.099609375 to 1
- w_expert: bfloat16 [16, 3584, 1536], P(('group', 'local')), may hold values from -0.09375 to 0.09375
Outputs:
- mixture: bfloat16 [4096, 1536], P(('parts', 'group', 'local')), parts along dimension 0
There are 2 independent parts, one for each index of `parts`. A program takes and returns all parts, laid end to end along the dimension named above; an argument that names none is the same for every part. Nothing has to cross between parts.
Inputs may be any that keep to these rules, and one draw needn't show every extreme that they name: `routes`: A row names 8 different experts lying in 4 node groups (expert e lies in group e // 4), two in each; the rows of one device name every expert exactly 64 times, and so each node group in exactly 128 rows.
All inputs are finite; a program needn't handle non-finite values.
Results may differ from a plain program's by a relative error of at most 0.008.
Values may be sent and summed in bfloat16 or wider, within the bound.
A program may use at most 128 MiB of HBM per device.

v0:
```python
import jax
import jax.numpy as jnp
from jax import lax
from jax.sharding import PartitionSpec as P


def shards(tokens, routes, gate_weights, w_expert):
    tok_rows, picks = routes.shape
    groups = lax.axis_size("group")
    per_group = lax.axis_size("local")
    experts = groups * per_group
    capacity = tok_rows * picks // experts
    weight = w_expert[0]
    gates = gate_weights.astype(jnp.float32)
    group_of = routes // per_group
    pick_ids = jnp.arange(picks, dtype=jnp.int32)
    same = group_of[:, :, None] == group_of[:, None, :]
    others = same & (pick_ids[:, None] != pick_ids[None, :])[None, :, :]
    partner = jnp.sum(jnp.where(others, pick_ids[None, None, :], 0), axis=2)
    earlier = jnp.sum(
        jnp.where(same & (pick_ids[None, :] < pick_ids[:, None])[None, :, :], 1, 0), axis=2
    ).astype(jnp.int32)
    first = (earlier == 0)[:, :, None]
    flat_ids = routes.reshape(-1)
    onehot = (flat_ids[:, None] == jnp.arange(experts, dtype=jnp.int32)[None, :]).astype(jnp.int32)
    before = jnp.cumsum(onehot, axis=0) - onehot
    slot_of = flat_ids * capacity + jnp.sum(before * onehot, axis=1)
    pair_tokens = jnp.arange(tok_rows * picks, dtype=jnp.int32) // picks
    source = jnp.zeros((experts * capacity,), jnp.int32).at[slot_of].set(pair_tokens)
    outgoing = tokens[source]
    arrived = lax.all_to_all(
        outgoing.reshape(experts, capacity, -1),
        ("group", "local"),
        split_axis=0,
        concat_axis=0,
        tiled=True,
    )
    flatrows = arrived.reshape(-1, arrived.shape[-1])
    result = (
        jax.nn.silu(jnp.dot(flatrows, weight, preferred_element_type=jnp.float32))
        .astype(jnp.bfloat16)
        .reshape(experts, capacity, -1)
    )
    returned = lax.all_to_all(result, ("group", "local"), split_axis=0, concat_axis=0, tiled=True)
    pair_out = returned.reshape(experts * capacity, -1)[slot_of].reshape(tok_rows, picks, -1)
    weighted = gates[:, :, None] * pair_out.astype(jnp.float32)
    group_sum = (weighted + jnp.take_along_axis(weighted, partner[:, :, None], axis=1)).astype(
        jnp.bfloat16
    )
    return jnp.sum(
        jnp.where(first, group_sum.astype(jnp.float32), jnp.float32(0.0)), axis=1
    ).astype(jnp.bfloat16)


def solution(mesh):
    return jax.shard_map(
        shards,
        mesh=mesh,
        in_specs=(
            P(("parts", "group", "local"), None),
            P(("parts", "group", "local"), None),
            P(("parts", "group", "local"), None),
            P(("group", "local"), None, None),
        ),
        out_specs=P(("parts", "group", "local"), None),
        check_vma=False,
    )
```

profile of v0, /device:TPU:11, one launch (start us, length us, event | category | flops | bytes accessed | tf_op | source)
XLA Modules:
  0.0 317.8 jit_solution(11255814407745730776)
XLA Ops:
  0.0 0.9 copy.26
  0.9 0.1 eq.54
  1.0 0.1 eq.50
  1.1 0.7 add_select_fusion.1
  1.8 4.5 %reduce-window.6 = s32[16,8,128]{2,1,0:T(8,128)S(1)} reduce-window(s32[16,8,128]{2,1,0:T(8,128)S(1)} %fusion.9, s32[]{:T(128)} %constant.49.clone.1), window={size=1x1x128 pad=0_0x0_0x127_0}, to_apply=%region_1.2 | reduce-window | flops 2080768 | bytes 131076 | tf_op jit(solution)/shard_map/reduce-window
  6.4 0.1 copy.28
  6.7 0.1 copy.25
  6.8 0.1 mul.34
  7.0 4.3 %scatter_custom_fusion = s32[1024]{0:T(1024)S(1)} fusion(s32[1024]{0:T(1024)S(1)} %bitcast.53, s32[1024]{0:T(1024)S(1)} %add_select_fusion, s32[]{:T(128)} %constant.49.clone.1), kind=kCustom, calls=%fused_computation.51 | custom fusion | bytes 4100 | tf_op jit(solution)/shard_map/scatter | solution.py:29
  11.3 7.3 %gather_fusion = bf16[1024,3584]{1,0:T(8,128)(2,1)} fusion(bf16[128,3584]{1,0:T(8,128)(2,1)S(1)} %copy-done, s32[1024]{0:T(1024)S(1)} %fusion.13), kind=kCustom, calls=%fused_computation | custom fusion | bytes 14684160 | tf_op jit(solution)/shard_map/gather | solution.py:30
  18.6 166.5 %all_to_all.10 = bf16[16,64,3584]{2,1,0:T(8,128)(2,1)S(1)} all-to-all(bf16[16,64,3584]{2,1,0:T(8,128)(2,1)} %bitcast.47), channel_id=1, replica_groups=mesh['parts'=2,'group'=4,'local'=4] {'group','local'}, dimensions={0} | all-to-all | bytes 14680064 | tf_op jit(solution)/shard_map/all_to_all | solution.py:31
  185.1 13.5 %multiply_convert_fusion = bf16[1024,1536]{1,0:T(8,128)(2,1)} fusion(bf16[1024,3584]{1,0:T(8,128)(2,1)S(1)} %bitcast.48, bf16[1,3584,1536]{2,1,0:T(8,128)(2,1)S(1)} %copy-done.2), kind=kOutput, calls=%fused_computation.11 | convolution fusion | flops 11282153472 | bytes 21495808 | tf_op jit(solution)/shard_map/dot_general | solution.py:40
  198.6 5.8 %all-to-all-start.1 = ((bf16[16,64,1536]{2,1,0:T(8,128)(2,1)}), bf16[16,64,1536]{2,1,0:T(8,128)(2,1)}, u32[]{:S(2)}, u32[]{:S(2)}) async-start(bf16[16,64,1536]{2,1,0:T(8,128)(2,1)} %bitcast.49), calls=%async_computation.1 | async-start | bytes 6291456 | tf_op jit(solution)/shard_map/all_to_all | solution.py:44
  204.3 0.1 copy.24
  204.5 0.1 select_reduce_fusion.2
  204.6 0.1 copy.31
  204.7 0.1 reshape.134
  204.8 0.1 copy.23
  204.9 0.1 copy.30
  205.0 69.3 %all-to-all-done.1 = bf16[16,64,1536]{2,1,0:T(8,128)(2,1)} async-done(((bf16[16,64,1536]{2,1,0:T(8,128)(2,1)}), bf16[16,64,1536]{2,1,0:T(8,128)(2,1)}, u32[]{:S(2)}, u32[]{:S(2)}) %all-to-all-start.1) | async-done | bytes 3145760 | tf_op jit(solution)/shard_map/all_to_all | solution.py:44
  274.3 9.6 %gather_fusion.1 = bf16[1024,1536]{1,0:T(8,128)(2,1)} fusion(bf16[1024,1536]{1,0:T(8,128)(2,1)} %bitcast.8, s32[1024]{0:T(1024)S(1)} %broadcast_clamp_fusion), kind=kCustom, calls=%fused_computation.1 | custom fusion | bytes 6295552 | tf_op jit(solution)/shard_map/gather | solution.py:45
  283.9 5.0 %convert_multiply_fusion = f32[128,8,1536]{2,1,0:T(8,128)} fusion(bf16[1024,1536]{1,0:T(8,128)(2,1)} %gather_fusion.1, f32[128,8]{1,0:T(8,128)S(1)} %copy.24), kind=kLoop, calls=%fused_computation.6 | loop fusion | flops 3145728 | bytes 9441280 | tf_op jit(solution)/shard_map/mul | solution.py:46
  288.9 23.0 %gather_fusion.2 = f32[1024,1536]{1,0:T(8,128)} fusion(f32[128,8,1536]{2,1,0:T(8,128)} %convert_multiply_fusion, s32[1024]{0:T(1024)S(1)} %reshape.134), kind=kCustom, calls=%fused_computation.2 | custom fusion | bytes 12591104 | tf_op jit(solution)/shard_map/jit(take_along_axis)/gather | solution.py:47
  311.9 5.9 %select_reduce_fusion = bf16[128,1536]{1,0:T(8,128)(2,1)} fusion(f32[1024,1536]{1,0:T(8,128)} %gather_fusion.2, pred[128,8]{1,0:T(8,128)(4,1)S(1)} %copy.30, pred[128,8]{1,0:T(8,128)(4,1)S(1)} %copy.23, bf16[1024,1536]{1,0:T(8,128)(2,1)} %gather_fusion.1, f32[128,8]{1,0:T(8,128)S(1)} %copy.24), kind=kLoop, calls=%fused_computation.10 | loop fusion | flops 12386304 | bytes 9836544 | tf_op jit(solution)/shard_map/reduce_sum | solution.py:50
  (21 shorter events, 0.4 us)
Async XLA Ops:
  0.0 11.3 %copy-start = (bf16[128,3584]{1,0:T(8,128)(2,1)S(1)}, bf16[128,3584]{1,0:T(8,128)(2,1)}, u32[]{:S(2)}) copy-start(bf16[128,3584]{1,0:T(8,128)(2,1)} %param.4) | copy-start | bytes 2752516
  18.6 166.5 %copy-start.2 = (bf16[1,3584,1536]{2,1,0:T(8,128)(2,1)S(1)}, bf16[1,3584,1536]{2,1,0:T(8,128)(2,1)}, u32[]{:S(2)}) copy-start(bf16[1,3584,1536]{2,1,0:T(8,128)(2,1)} %param.7) | copy-start | bytes 33030148
  198.6 5.8 %copy-start.1 = (bf16[128,8]{0,1:T(8,128)(2,1)S(1)}, bf16[128,8]{0,1:T(8,128)(2,1)}, u32[]{:S(2)}) copy-start(bf16[128,8]{0,1:T(8,128)(2,1)} %param.6) | copy-start | bytes 6148
  198.6 75.7 %all-to-all-start.1 = ((bf16[16,64,1536]{2,1,0:T(8,128)(2,1)}), bf16[16,64,1536]{2,1,0:T(8,128)(2,1)}, u32[]{:S(2)}, u32[]{:S(2)}) async-start(bf16[16,64,1536]{2,1,0:T(8,128)(2,1)} %bitcast.49), calls=%async_computation.1 | async-start | bytes 6291456 | tf_op jit(solution)/shard_map/all_to_all | solution.py:44
where the time goes:
time: 318 us
  blocking collectives  166 us (52%)
  waiting for transfers between devices  69.3 us (22%)
  local copies, waits for them, and re-layouts  46.3 us (15%)
  other arithmetic  16.4 us (5%)
  matrix products  13.5 us (4%)
  starting transfers between devices  5.75 us (2%)
    all_to_all x1, blocking collectives, shards(): lax.all_to_all(outgoing.reshape(experts, capacity, -1), ('group', 'local'...  166 us
    all_to_all x1, waiting for transfers between devices, shards(): lax.all_to_all(result, ('group', 'local'), split_axis=0, concat_axis=0, t...  69.3 us
    gather x3, local copies, waits for them, and re-layouts, shards(): jnp.take_along_axis(weighted, partner[:, :, None], axis=1)  23.2 us
    dot_general x1, matrix products, shards(): jnp.dot(flatrows, weight, preferred_element_type=jnp.float32)  13.5 us
    gather x1, local copies, waits for them, and re-layouts, shards(): returned.reshape(experts * capacity, -1)[slot_of]  9.57 us
    gather x1, local copies, waits for them, and re-layouts, shards(): outgoing = tokens[source]  7.32 us
  transfers between devices with their start and end apart: 1, of which 1 were waited for; matrix products, arithmetic and copies ran while one was open for 0% of the time, Pallas kernels for 0%

commit v1 on v0

--- a/solution.py
+++ b/solution.py
@@ -1,10 +1,16 @@
+import functools
+
 import jax
 import jax.numpy as jnp
 from jax import lax
+from jax.experimental import pallas as pl
+from jax.experimental.pallas import tpu as pltpu
 from jax.sharding import PartitionSpec as P
 
-
-def shards(tokens, routes, gate_weights, w_expert):
+SPEC = P(("parts", "group", "local"), None)
+
+
+def routed(tokens, routes, gate_weights, w_expert):
     tok_rows, picks = routes.shape
     groups = lax.axis_size("group")
     per_group = lax.axis_size("local")
@@ -52,16 +58,302 @@
     ).astype(jnp.bfloat16)
 
 
+def tile_of(width, most):
+    tile = most
+    while width % tile:
+        tile -= 128
+    return tile
+
+
+def fused_kernel(
+    G, L, cap,
+    tok_ref, meta_ref, w_ref, out_ref,
+    w, tok, meta, pick, comb, sel, rows, outs, res, gsum, gin,
+    load_sem, meta_s, meta_r, up_s, down_s, tok_r, row_s, row_r, res_s, res_r, gs_s, gs_r,
+):
+    T, D = tok_ref.shape
+    FF = w_ref.shape[1]
+    picks = meta_ref.shape[0] // 2
+    g = lax.axis_index("group")
+    l = lax.axis_index("local")
+
+    low = jnp.minimum(g, G - 1 - g)
+    side = jnp.where(g < G - 1 - g, 1, -1)
+
+    def origin(i):
+        near = (i + 1) // 2 * jnp.where(i % 2 == 1, -1, 1)
+        return g + jnp.where(i <= 2 * low, near, (i - low) * side)
+
+    def far(k):
+        return lax.rem(g + k, G)
+
+    def peer(k):
+        return lax.rem(l + k, L)
+
+    def remote(src, dst, send, recv, group=None, local=None):
+        where = {}
+        if group is not None:
+            where["group"] = group
+        if local is not None:
+            where["local"] = local
+        return pltpu.make_async_remote_copy(
+            src_ref=src, dst_ref=dst, send_sem=send, recv_sem=recv,
+            device_id=where, device_id_type=pl.DeviceIdType.MESH,
+        )
+
+    def meta_copy(k):
+        return remote(meta.at[g], meta.at[g], meta_s.at[k], meta_r.at[g], group=far(k))
+
+    def up_copy(o):
+        return remote(tok.at[o], tok.at[o], up_s.at[o], tok_r.at[o], group=g + 1)
+
+    def down_copy(o):
+        return remote(tok.at[o], tok.at[o], down_s.at[o], tok_r.at[o], group=g - 1)
+
+    def row_copy(o, k):
+        e = peer(k)
+        return remote(sel.at[o, e], rows.at[o, l], row_s.at[o, e], row_r.at[o, l], local=e)
+
+    def res_copy(o, k):
+        e = peer(k)
+        return remote(outs.at[o, e], res.at[o, l], res_s.at[o, e], res_r.at[o, l], local=e)
+
+    def gs_copy(o):
+        return remote(gsum.at[o], gin.at[g], gs_s.at[o], gs_r.at[g], group=o)
+
+    load_meta = pltpu.make_async_copy(meta_ref, meta.at[g], load_sem.at[0])
+    load_tok = pltpu.make_async_copy(tok_ref, tok.at[g], load_sem.at[1])
+    load_w = pltpu.make_async_copy(w_ref, w, load_sem.at[2])
+    load_meta.start()
+    load_tok.start()
+    load_w.start()
+
+    barrier = pltpu.get_barrier_semaphore()
+    for k in range(1, G):
+        pl.semaphore_signal(
+            barrier, inc=1, device_id={"group": far(k)}, device_id_type=pl.DeviceIdType.MESH
+        )
+    for k in range(1, L):
+        pl.semaphore_signal(
+            barrier, inc=1, device_id={"local": peer(k)}, device_id_type=pl.DeviceIdType.MESH
+        )
+    pl.semaphore_wait(barrier, G + L - 2)
+
+    load_meta.wait()
+    for k in range(1, G):
+        meta_copy(k).start()
+    load_tok.wait()
+
+    def arrive(i):
+        o = origin(i)
+
+        @pl.when(o != g)
+        def _():
+            pltpu.make_async_copy(tok.at[o], tok.at[o], tok_r.at[o]).wait()
+
+        @pl.when((o <= g) & (g < G - 1))
+        def _():
+            up_copy(o).start()
+
+        @pl.when((o >= g) & (g > 0))
+        def _():
+            down_copy(o).start()
+
+        @pl.when(o != g)
+        def _():
+            pltpu.make_async_copy(meta.at[o], meta.at[o], meta_r.at[o]).wait()
+
+        chosen = meta[o, 0:picks, :]
+        gates = meta[o, picks : 2 * picks, :]
+        line = lax.broadcasted_iota(jnp.int32, (picks, T), 0)
+        members = jnp.zeros((picks, T), jnp.float32)
+        mine, scale = [], []
+        for e in range(L):
+            hit = chosen == (g * L + e).astype(jnp.float32)
+            mine.append(jnp.sum(jnp.where(hit, 1.0, 0.0), axis=0, keepdims=True))
+            scale.append(jnp.sum(jnp.where(hit, gates, 0.0), axis=0, keepdims=True))
+            members = members + jnp.where(line == e, mine[e], 0.0)
+        ahead = jnp.where(
+            lax.broadcasted_iota(jnp.int32, (T, T), 0) < lax.broadcasted_iota(jnp.int32, (T, T), 1),
+            1.0, 0.0,
+        )
+        rank = jnp.dot(members, ahead, preferred_element_type=jnp.float32)
+        slot = lax.broadcasted_iota(jnp.int32, (cap, T), 0).astype(jnp.float32)
+        for e in range(L):
+            here = jnp.where((slot == rank[e : e + 1, :]) & (mine[e] > 0.5), 1.0, 0.0)
+            pick[o, e * cap : (e + 1) * cap, :] = here.astype(jnp.bfloat16)
+            comb[o, e * cap : (e + 1) * cap, :] = here * scale[e]
+
+        tile = tile_of(D, 512)
+
+        def part(n, carry):
+            at = pl.ds(pl.multiple_of(n * tile, tile), tile)
+            got = jnp.dot(pick[o], tok[o, :, at], preferred_element_type=jnp.float32)
+            sel[o, :, :, at] = got.astype(jnp.bfloat16).reshape(L, cap, tile)
+            return carry
+
+        lax.fori_loop(0, D // tile, part, 0)
+        for k in range(1, L):
+            row_copy(o, k).start()
+        keep = pltpu.make_async_copy(sel.at[o, l], rows.at[o, l], row_r.at[o, l])
+        keep.start()
+
+    def expert(i):
+        o = origin(i)
+        for k in range(L):
+            e = peer(k)
+            pltpu.make_async_copy(rows.at[o, e], rows.at[o, e], row_r.at[o, e]).wait()
+        tile = tile_of(FF, 512)
+
+        def part(n, carry):
+            at = pl.ds(pl.multiple_of(n * tile, tile), tile)
+            v = jnp.dot(
+                rows[o].reshape(L * cap, D), w[:, at], preferred_element_type=jnp.float32
+            )
+            v = v / (1.0 + jnp.exp(-v))
+            outs[o, :, :, at] = v.astype(jnp.bfloat16).reshape(L, cap, tile)
+            return carry
+
+        lax.fori_loop(0, FF // tile, part, 0)
+        for k in range(1, L):
+            res_copy(o, k).start()
+        keep = pltpu.make_async_copy(outs.at[o, l], res.at[o, l], res_r.at[o, l])
+        keep.start()
+
+    def combine(i):
+        o = origin(i)
+        for k in range(L):
+            e = peer(k)
+            pltpu.make_async_copy(res.at[o, e], res.at[o, e], res_r.at[o, e]).wait()
+        tile = tile_of(FF, 512)
+        back = jnp.transpose(comb[o]).astype(jnp.bfloat16)
+
+        def part(n, carry):
+            at = pl.ds(pl.multiple_of(n * tile, tile), tile)
+            got = jnp.dot(
+                back, res[o, :, :, at].reshape(L * cap, tile), preferred_element_type=jnp.float32
+            )
+            gsum[o, :, at] = got.astype(jnp.bfloat16)
+            return carry
+
+        lax.fori_loop(0, FF // tile, part, 0)
+
+        @pl.when(o != g)
+        def _():
+            gs_copy(o).start()
+
+    def step(i, carry):
+        @pl.when(i < G)
+        def _():
+            arrive(i)
+
+        @pl.when((i >= 1) & (i < G + 1))
+        def _():
+            @pl.when(i == 1)
+            def _():
+                load_w.wait()
+
+            expert(i - 1)
+
+        @pl.when(i >= 2)
+        def _():
+            combine(i - 2)
+
+        return carry
+
+    lax.fori_loop(0, G + 2, step, 0)
+
+    total = gsum[g].astype(jnp.float32)
+    for k in range(1, G):
+        o = far(k)
+        pltpu.make_async_copy(gin.at[o], gin.at[o], gs_r.at[o]).wait()
+        total = total + gin[o].astype(jnp.float32)
+    out_ref[...] = total.astype(out_ref.dtype)
+
+    for k in range(1, G):
+        meta_copy(k).wait_send()
+        gs_copy(far(k)).wait_send()
+
+    def drain(o, carry):
+        @pl.when((o <= g) & (g < G - 1))
+        def _():
+            up_copy(o).wait_send()
+
+        @pl.when((o >= g) & (g > 0))
+        def _():
+            down_copy(o).wait_send()
+
+        for k in range(1, L):
+            row_copy(o, k).wait_send()
+            res_copy(o, k).wait_send()
+        return carry
+
+    lax.fori_loop(0, G, drain, 0)
+
+
+def everywhere(tokens, routes, gate_weights, w_expert):
+    T, D = tokens.shape
+    picks = routes.shape[1]
+    G = lax.axis_size("group")
+    L = lax.axis_size("local")
+    cap = T * picks // (G * L)
+    FF = w_expert.shape[2]
+    meta = jnp.concatenate(
+        [routes.T.astype(jnp.float32), gate_weights.T.astype(jnp.float32)], axis=0
+    )
+    dma = pltpu.SemaphoreType.DMA
+    bf16 = jnp.bfloat16
+    return pl.pallas_call(
+        functools.partial(fused_kernel, G, L, cap),
+        out_shape=jax.ShapeDtypeStruct((T, FF), bf16),
+        in_specs=[pl.BlockSpec(memory_space=pl.ANY)] * 3,
+        out_specs=pl.BlockSpec(memory_space=pltpu.VMEM),
+        scratch_shapes=[
+            pltpu.VMEM((D, FF), bf16),
+            pltpu.VMEM((G, T, D), bf16),
+            pltpu.VMEM((G, 2 * picks, T), jnp.float32),
+            pltpu.VMEM((G, L * cap, T), bf16),
+            pltpu.VMEM((G, L * cap, T), jnp.float32),
+            pltpu.VMEM((G, L, cap, D), bf16),
+            pltpu.VMEM((G, L, cap, D), bf16),
+            pltpu.VMEM((G, L, cap, FF), bf16),
+            pltpu.VMEM((G, L, cap, FF), bf16),
+            pltpu.VMEM((G, T, FF), bf16),
+            pltpu.VMEM((G, T, FF), bf16),
+            dma((3,)),
+            dma((G,)),
+            dma((G,)),
+            dma((G,)),
+            dma((G,)),
+            dma((G,)),
+            dma((G, L)),
+            dma((G, L)),
+            dma((G, L)),
+            dma((G, L)),
+            dma((G,)),
+            dma((G,)),
+        ],
+        compiler_params=pltpu.CompilerParams(
+            collective_id=0, has_side_effects=True, vmem_limit_bytes=58 * 1024 * 1024
+        ),
+        cost_estimate=pl.CostEstimate(
+            flops=2 * T * picks * D * FF, bytes_accessed=2 * D * FF, transcendentals=T * picks * FF
+        ),
+    )(tokens, meta, w_expert[0])
+
+
 def solution(mesh):
+    groups = mesh.shape["group"]
+
+    def shards(tokens, routes, gate_weights, w_expert):
+        if routes.shape[1] == 2 * groups:
+            return everywhere(tokens, routes, gate_weights, w_expert)
+        return routed(tokens, routes, gate_weights, w_expert)
+
     return jax.shard_map(
         shards,
         mesh=mesh,
-        in_specs=(
-            P(("parts", "group", "local"), None),
-            P(("parts", "group", "local"), None),
-            P(("parts", "group", "local"), None),
-            P(("group", "local"), None, None),
-        ),
-        out_specs=P(("parts", "group", "local"), None),
+        in_specs=(SPEC, SPEC, SPEC, P(("group", "local"), None, None)),
+        out_specs=SPEC,
         check_vma=False,
     )

time: 318 us -> 152 us (0.48)
  the two profiles are of different devices: /device:TPU:11 before, /device:TPU:25 now
where the time goes in v1:
time: 152 us
  Pallas kernels  148 us (97%)
  other arithmetic  1.97 us (1%)
  local copies, waits for them, and re-layouts  1.77 us (1%)
    pallas_call x1, Pallas kernels, everywhere(): pl.pallas_call(functools.partial(fused_kernel, G, L, cap), out_shape=jax....  148 us

profile of v1, /device:TPU:25, one launch (start us, length us, event | category | flops | bytes accessed | tf_op | source)
XLA Modules:
  0.0 151.5 jit_solution(3392937663052785219)
XLA Ops:
  0.0 0.7 convert_bitcast_fusion.1
  0.7 0.7 convert_bitcast_fusion
  1.4 0.6 pad_maximum_fusion.meta_ref
  2.0 147.8 %shard_map.46 = bf16[128,1536]{1,0:T(8,128)(2,1)} custom-call(bf16[128,3584]{1,0:T(8,128)(2,1)} %tok_ref.1, f32[16,128]{1,0:T(8,128)} %pad_maximum_fusion.meta_ref, bf16[3584,1536]{1,0:T(8,128)(2,1)} %bitcast.5), custom_call_target="tpu_custom_call" | custom-call | flops 11274289152 | bytes 11010048 | tf_op jit(solution)/shard_map/pallas_call | solution.py:306
  149.8 1.8 %copy.6 = bf16[128,1536]{1,0:T(8,128)(2,1)} copy(bf16[128,1536]{1,0:T(8,128)(2,1)} %shard_map.46) | data formatting | bytes 786432

commit v2 on v1

v2 whole, which is shorter than its diff:
```python
import functools

import jax
import jax.numpy as jnp
from jax import lax
from jax.experimental import pallas as pl
from jax.experimental.pallas import tpu as pltpu
from jax.sharding import PartitionSpec as P

WIDE = 2

SPEC = P(("parts", "group", "local"), None)


def routed(tokens, routes, gate_weights, w_expert):
    tok_rows, picks = routes.shape
    groups = lax.axis_size("group")
    per_group = lax.axis_size("local")
    experts = groups * per_group
    capacity = tok_rows * picks // experts
    weight = w_expert[0]
    gates = gate_weights.astype(jnp.float32)
    group_of = routes // per_group
    pick_ids = jnp.arange(picks, dtype=jnp.int32)
    same = group_of[:, :, None] == group_of[:, None, :]
    others = same & (pick_ids[:, None] != pick_ids[None, :])[None, :, :]
    partner = jnp.sum(jnp.where(others, pick_ids[None, None, :], 0), axis=2)
    earlier = jnp.sum(
        jnp.where(same & (pick_ids[None, :] < pick_ids[:, None])[None, :, :], 1, 0), axis=2
    ).astype(jnp.int32)
    first = (earlier == 0)[:, :, None]
    flat_ids = routes.reshape(-1)
    onehot = (flat_ids[:, None] == jnp.arange(experts, dtype=jnp.int32)[None, :]).astype(jnp.int32)
    before = jnp.cumsum(onehot, axis=0) - onehot
    slot_of = flat_ids * capacity + jnp.sum(before * onehot, axis=1)
    pair_tokens = jnp.arange(tok_rows * picks, dtype=jnp.int32) // picks
    source = jnp.zeros((experts * capacity,), jnp.int32).at[slot_of].set(pair_tokens)
    outgoing = tokens[source]
    arrived = lax.all_to_all(
        outgoing.reshape(experts, capacity, -1),
        ("group", "local"),
        split_axis=0,
        concat_axis=0,
        tiled=True,
    )
    flatrows = arrived.reshape(-1, arrived.shape[-1])
    result = (
        jax.nn.silu(jnp.dot(flatrows, weight, preferred_element_type=jnp.float32))
        .astype(jnp.bfloat16)
        .reshape(experts, capacity, -1)
    )
    returned = lax.all_to_all(result, ("group", "local"), split_axis=0, concat_axis=0, tiled=True)
    pair_out = returned.reshape(experts * capacity, -1)[slot_of].reshape(tok_rows, picks, -1)
    weighted = gates[:, :, None] * pair_out.astype(jnp.float32)
    group_sum = (weighted + jnp.take_along_axis(weighted, partner[:, :, None], axis=1)).astype(
        jnp.bfloat16
    )
    return jnp.sum(
        jnp.where(first, group_sum.astype(jnp.float32), jnp.float32(0.0)), axis=1
    ).astype(jnp.bfloat16)


def tile_of(width, most):
    tile = most
    while width % tile:
        tile -= 128
    return tile


def fused_kernel(
    G, L, cap, W, WF, wide,
    tok_ref, meta_ref, w_ref, out_ref,
    w, tok, tokx, meta, metax, pick, pickx, comb, sel, selx, rows, outs, res, gsum, gin,
    load_sem, meta_s, meta_r, metax_s, metax_r, cross_s,
    up_s, down_s, tok_r, upx_s, downx_s, tokx_r,
    row_s, rowx_s, row_r, res_s, res_r, gs_s, gs_r,
):
    T, D = tok_ref.shape
    FF = w_ref.shape[1]
    C, N, H = D // W, FF // WF, L // 2
    narrow = C - wide
    picks = meta_ref.shape[0] // 2
    g = lax.axis_index("group")
    l = lax.axis_index("local")
    base = l // H * H
    across = lax.rem(l + H, L)

    low = jnp.minimum(g, G - 1 - g)
    side = jnp.where(g < G - 1 - g, 1, -1)

    def origin(i):
        near = (i + 1) // 2 * jnp.where(i % 2 == 1, -1, 1)
        return g + jnp.where(i <= 2 * low, near, (i - low) * side)

    def far(k):
        return lax.rem(g + k, G)

    def mate(k):
        return base + lax.rem(l - base + k, H)

    def away(k):
        return lax.rem(base + H, L) + k

    def remote(src, dst, send, recv, group=None, local=None):
        where = {}
        if group is not None:
            where["group"] = group
        if local is not None:
            where["local"] = local
        return pltpu.make_async_remote_copy(
            src_ref=src, dst_ref=dst, send_sem=send, recv_sem=recv,
            device_id=where, device_id_type=pl.DeviceIdType.MESH,
        )

    def wait_for(ref, sem):
        pltpu.make_async_copy(ref, ref, sem).wait()

    def meta_copy(k):
        return remote(meta.at[g], meta.at[g], meta_s.at[k], meta_r.at[g], group=far(k))

    def metax_copy(k):
        return remote(
            meta.at[g], metax.at[g], metax_s.at[k], metax_r.at[g], group=far(k), local=across
        )

    load_meta = pltpu.make_async_copy(meta_ref, meta.at[g], load_sem.at[0])
    load_w = pltpu.make_async_copy(w_ref, w, load_sem.at[1])
    load_meta.start()
    for c in range(C):
        pltpu.make_async_copy(
            tok_ref.at[:, pl.ds(c * W, W)], tok.at[g, c], tok_r.at[g, c]
        ).start()
    load_w.start()

    barrier = pltpu.get_barrier_semaphore()
    greeted = 0
    for k in range(1, G):
        for where in ({"group": far(k)}, {"group": far(k), "local": across}):
            pl.semaphore_signal(
                barrier, inc=1, device_id=where, device_id_type=pl.DeviceIdType.MESH
            )
            greeted += 1
    for k in range(1, L):
        pl.semaphore_signal(
            barrier, inc=1, device_id={"local": lax.rem(l + k, L)},
            device_id_type=pl.DeviceIdType.MESH,
        )
        greeted += 1
    pl.semaphore_wait(barrier, greeted)

    load_meta.wait()
    if wide:
        metax_copy(0).start()
    for k in range(1, G):
        meta_copy(k).start()
        if wide:
            metax_copy(k).start()

    def places(info, first, count):
        chosen = info[0:picks, :]
        gates = info[picks : 2 * picks, :]
        line = lax.broadcasted_iota(jnp.int32, (picks, T), 0)
        members = jnp.zeros((picks, T), jnp.float32)
        mine, scale = [], []
        for e in range(count):
            hit = chosen == (first + e).astype(jnp.float32)
            mine.append(jnp.sum(jnp.where(hit, 1.0, 0.0), axis=0, keepdims=True))
            scale.append(jnp.sum(jnp.where(hit, gates, 0.0), axis=0, keepdims=True))
            members = members + jnp.where(line == e, mine[e], 0.0)
        ahead = jnp.where(
            lax.broadcasted_iota(jnp.int32, (T, T), 0) < lax.broadcasted_iota(jnp.int32, (T, T), 1),
            1.0, 0.0,
        )
        rank = jnp.dot(members, ahead, preferred_element_type=jnp.float32)
        slot = lax.broadcasted_iota(jnp.int32, (cap, T), 0).astype(jnp.float32)
        here = [
            jnp.where((slot == rank[e : e + 1, :]) & (mine[e] > 0.5), 1.0, 0.0)
            for e in range(count)
        ]
        return here, scale

    def pass_on(buf, o, c, up, down, recv):
        @pl.when((o <= g) & (g < G - 1))
        def _():
            remote(buf.at[o, c], buf.at[o, c], up.at[o], recv.at[o, c], group=g + 1).start()

        @pl.when((o >= g) & (g > 0))
        def _():
            remote(buf.at[o, c], buf.at[o, c], down.at[o], recv.at[o, c], group=g - 1).start()

    def arrive(i):
        o = origin(i)

        @pl.when(o != g)
        def _():
            wait_for(meta.at[o], meta_r.at[o])

        here, scale = places(meta[o], g * L, L)
        for e in range(L):
            pick[o, e * cap : (e + 1) * cap, :] = here[e].astype(jnp.bfloat16)
            comb[o, e * cap : (e + 1) * cap, :] = here[e] * scale[e]

        def chunk(c, carry):
            @pl.when(o != g)
            def _():
                wait_for(tok.at[o, c], tok_r.at[o, c])

            pass_on(tok, o, c, up_s, down_s, tok_r)
            got = jnp.dot(pick[o], tok[o, c], preferred_element_type=jnp.float32)
            sel[o, c] = got.astype(jnp.bfloat16).reshape(L, cap, W)

            @pl.when(c < narrow)
            def _():
                for k in range(H):
                    e = away(k)
                    remote(
                        sel.at[o, c, e], rows.at[o, c, l], row_s.at[o, e], row_r.at[o, l], local=e
                    ).start()

            for k in range(1, H):
                e = mate(k)
                remote(
                    sel.at[o, c, e], rows.at[o, c, l], row_s.at[o, e], row_r.at[o, l], local=e
                ).start()
            rows[o, c, l] = sel[o, c, l]
            return carry

        lax.fori_loop(0, C, chunk, 0)

        if wide:
            wait_for(metax.at[o], metax_r.at[o])
            here, _ = places(metax[o], g * L + base, H)
            for e in range(H):
                pickx[e * cap : (e + 1) * cap, :] = here[e].astype(jnp.bfloat16)

            def chunkx(c, carry):
                wait_for(tokx.at[o, c], tokx_r.at[o, c])
                pass_on(tokx, o, c, upx_s, downx_s, tokx_r)
                got = jnp.dot(pickx[...], tokx[o, c], preferred_element_type=jnp.float32)
                selx[o, c] = got.astype(jnp.bfloat16).reshape(H, cap, W)
                for k in range(1, H):
                    e = mate(k)
                    remote(
                        selx.at[o, c, e - base], rows.at[o, narrow + c, across],
                        rowx_s.at[o, e - base], row_r.at[o, across], local=e,
                    ).start()
                rows[o, narrow + c, across] = selx[o, c, l - base]
                return carry

            lax.fori_loop(0, wide, chunkx, 0)

    def expert(i):
        o = origin(i)
        for k in range(1, H):
            wait_for(rows.at[o, :, mate(k)], row_r.at[o, mate(k)])
            other = lax.rem(mate(k) + H, L)
            wait_for(rows.at[o, :, other], row_r.at[o, other])
        wait_for(rows.at[o, pl.ds(0, narrow), across], row_r.at[o, across])

        def part(n, carry):
            at = pl.ds(pl.multiple_of(n * WF, WF), WF)
            v = jnp.zeros((L * cap, WF), jnp.float32)
            for c in range(C):
                v = v + jnp.dot(
                    rows[o, c].reshape(L * cap, W), w[c * W : (c + 1) * W, at],
                    preferred_element_type=jnp.float32,
                )
            v = v / (1.0 + jnp.exp(-v))
            outs[o, n] = v.astype(jnp.bfloat16).reshape(L, cap, WF)
            for k in range(1, L):
                e = lax.rem(l + k, L)
                remote(
                    outs.at[o, n, e], res.at[o, n, l], res_s.at[o, e], res_r.at[o, n, l], local=e
                ).start()
            res[o, n, l] = outs[o, n, l]
            return carry

        lax.fori_loop(0, N, part, 0)

    def combine(i):
        o = origin(i)
        back = jnp.transpose(comb[o]).astype(jnp.bfloat16)

        def part(n, carry):
            for k in range(1, L):
                e = lax.rem(l + k, L)
                wait_for(res.at[o, n, e], res_r.at[o, n, e])
            got = jnp.dot(
                back, res[o, n].reshape(L * cap, WF), preferred_element_type=jnp.float32
            )
            gsum[o, n] = got.astype(jnp.bfloat16)

            @pl.when(o != g)
            def _():
                remote(
                    gsum.at[o, n], gin.at[g, n], gs_s.at[o], gs_r.at[g, n], group=o
                ).start()

            return carry

        lax.fori_loop(0, N, part, 0)

    for c in range(C):
        wait_for(tok.at[g, c], tok_r.at[g, c])
    for c in range(wide):
        remote(
            tok.at[g, narrow + c], tokx.at[g, c], cross_s, tokx_r.at[g, c], local=across
        ).start()

    def step(i, carry):
        @pl.when(i < G)
        def _():
            arrive(i)

        @pl.when((i >= 1) & (i < G + 1))
        def _():
            @pl.when(i == 1)
            def _():
                load_w.wait()

            expert(i - 1)

        @pl.when(i >= 2)
        def _():
            combine(i - 2)

        return carry

    lax.fori_loop(0, G + 2, step, 0)

    for n in range(N):
        total = gsum[g, n].astype(jnp.float32)
        for k in range(1, G):
            o = far(k)
            wait_for(gin.at[o, n], gs_r.at[o, n])
            total = total + gin[o, n].astype(jnp.float32)
        out_ref[:, n * WF : (n + 1) * WF] = total.astype(out_ref.dtype)

    if wide:
        metax_copy(0).wait_send()
    for k in range(1, G):
        meta_copy(k).wait_send()
        if wide:
            metax_copy(k).wait_send()
        wait_for(gsum.at[far(k)], gs_s.at[far(k)])
    if wide:
        wait_for(tokx.at[g], cross_s)

    def drain(o, carry):
        @pl.when((o <= g) & (g < G - 1))
        def _():
            wait_for(tok.at[o], up_s.at[o])
            if wide:
                wait_for(tokx.at[o], upx_s.at[o])

        @pl.when((o >= g) & (g > 0))
        def _():
            wait_for(tok.at[o], down_s.at[o])
            if wide:
                wait_for(tokx.at[o], downx_s.at[o])

        for k in range(H):
            wait_for(sel.at[o, pl.ds(0, narrow), away(k)], row_s.at[o, away(k)])
        for k in range(1, H):
            wait_for(sel.at[o, :, mate(k)], row_s.at[o, mate(k)])
            if wide:
                wait_for(selx.at[o, :, mate(k) - base], rowx_s.at[o, mate(k) - base])
        for k in range(1, L):
            e = lax.rem(l + k, L)
            wait_for(outs.at[o, :, e], res_s.at[o, e])
        return carry

    lax.fori_loop(0, G, drain, 0)


def everywhere(tokens, routes, gate_weights, w_expert):
    T, D = tokens.shape
    picks = routes.shape[1]
    G = lax.axis_size("group")
    L = lax.axis_size("local")
    cap = T * picks // (G * L)
    FF = w_expert.shape[2]
    W, WF = tile_of(D, 512), tile_of(FF, 512)
    C, N, H = D // W, FF // WF, L // 2
    wide = C * WIDE // 7
    some = max(wide, 1)
    meta = jnp.concatenate(
        [routes.T.astype(jnp.float32), gate_weights.T.astype(jnp.float32)], axis=0
    )
    dma = pltpu.SemaphoreType.DMA
    bf16 = jnp.bfloat16
    return pl.pallas_call(
        functools.partial(fused_kernel, G, L, cap, W, WF, wide),
        out_shape=jax.ShapeDtypeStruct((T, FF), bf16),
        in_specs=[pl.BlockSpec(memory_space=pl.ANY)] * 3,
        out_specs=pl.BlockSpec(memory_space=pltpu.VMEM),
        scratch_shapes=[
            pltpu.VMEM((D, FF), bf16),
            pltpu.VMEM((G, C, T, W), bf16),
            pltpu.VMEM((G, some, T, W), bf16),
            pltpu.VMEM((G, 2 * picks, T), jnp.float32),
            pltpu.VMEM((G, 2 * picks, T), jnp.float32),
            pltpu.VMEM((G, L * cap, T), bf16),
            pltpu.VMEM((H * cap, T), bf16),
            pltpu.VMEM((G, L * cap, T), jnp.float32),
            pltpu.VMEM((G, C, L, cap, W), bf16),
            pltpu.VMEM((G, some, H, cap, W), bf16),
            pltpu.VMEM((G, C, L, cap, W), bf16),
            pltpu.VMEM((G, N, L, cap, WF), bf16),
            pltpu.VMEM((G, N, L, cap, WF), bf16),
            pltpu.VMEM((G, N, T, WF), bf16),
            pltpu.VMEM((G, N, T, WF), bf16),
            dma((2,)),
            dma((G,)),
            dma((G,)),
            dma((G,)),
            dma((G,)),
            dma,
            dma((G,)),
            dma((G,)),
            dma((G, C)),
            dma((G,)),
            dma((G,)),
            dma((G, some)),
            dma((G, L)),
            dma((G, H)),
            dma((G, L)),
            dma((G, L)),
            dma((G, N, L)),
            dma((G,)),
            dma((G, N)),
        ],
        compiler_params=pltpu.CompilerParams(
            collective_id=0, has_side_effects=True, vmem_limit_bytes=58 * 1024 * 1024
        ),
        cost_estimate=pl.CostEstimate(
            flops=2 * T * picks * D * FF, bytes_accessed=2 * D * FF, transcendentals=T * picks * FF
        ),
    )(tokens, meta, w_expert[0])


def solution(mesh):
    groups = mesh.shape["group"]

    def shards(tokens, routes, gate_weights, w_expert):
        if routes.shape[1] == 2 * groups:
            return everywhere(tokens, routes, gate_weights, w_expert)
        return routed(tokens, routes, gate_weights, w_expert)

    return jax.shard_map(
        shards,
        mesh=mesh,
        in_specs=(SPEC, SPEC, SPEC, P(("group", "local"), None, None)),
        out_specs=SPEC,
        check_vma=False,
    )
```

time: 152 us -> 130 us (0.86)
  the two profiles are of different devices: /device:TPU:25 before, /device:TPU:0 now
where the time goes in v2:
time: 130 us; the launch traced here: 129 us
  Pallas kernels  126 us (97%)
  other arithmetic  1.97 us (2%)
  local copies, waits for them, and re-layouts  1.77 us (1%)
    pallas_call x1, Pallas kernels, everywhere(): pl.pallas_call(functools.partial(fused_kernel, G, L, cap, W, WF, wide), o...  126 us

profile of v2, /device:TPU:0, one launch (start us, length us, event | category | flops | bytes accessed | tf_op | source)
XLA Modules:
  0.0 129.4 jit_solution(3633445415293845007)
XLA Ops:
  0.0 0.7 convert_bitcast_fusion.1
  0.7 0.7 convert_bitcast_fusion
  1.4 0.6 pad_maximum_fusion.meta_ref
  2.0 125.7 %shard_map.46 = bf16[128,1536]{1,0:T(8,128)(2,1)} custom-call(bf16[128,3584]{1,0:T(8,128)(2,1)} %tok_ref.1, f32[16,128]{1,0:T(8,128)} %pad_maximum_fusion.meta_ref, bf16[3584,1536]{1,0:T(8,128)(2,1)} %bitcast.5), custom_call_target="tpu_custom_call" | custom-call | flops 11274289152 | bytes 11010048 | tf_op jit(solution)/shard_map/pallas_call | solution.py:392
  127.7 1.8 %copy.6 = bf16[128,1536]{1,0:T(8,128)(2,1)} copy(bf16[128,1536]{1,0:T(8,128)(2,1)} %shard_map.46) | data formatting | bytes 786432

commit v3 on v2

--- a/solution.py
+++ b/solution.py
@@ -7,7 +7,7 @@
 from jax.experimental.pallas import tpu as pltpu
 from jax.sharding import PartitionSpec as P
 
-WIDE = 2
+WIDE = 5
 
 SPEC = P(("parts", "group", "local"), None)
 
@@ -380,9 +380,9 @@
     L = lax.axis_size("local")
     cap = T * picks // (G * L)
     FF = w_expert.shape[2]
-    W, WF = tile_of(D, 512), tile_of(FF, 512)
+    W, WF = tile_of(D, 256), tile_of(FF, 512)
     C, N, H = D // W, FF // WF, L // 2
-    wide = C * WIDE // 7
+    wide = C * WIDE // 14
     some = max(wide, 1)
     meta = jnp.concatenate(
         [routes.T.astype(jnp.float32), gate_weights.T.astype(jnp.float32)], axis=0

time: 130 us -> 128 us (0.985)
  Pallas kernels: 126 us -> 124 us
where the time goes in v3:
time: 128 us
  Pallas kernels  124 us (97%)
  other arithmetic  1.97 us (2%)
  local copies, waits for them, and re-layouts  1.77 us (1%)
    pallas_call x1, Pallas kernels, everywhere(): pl.pallas_call(functools.partial(fused_kernel, G, L, cap, W, WF, wide), o...  124 us

profile of v3, /device:TPU:0, one launch (start us, length us, event | category | flops | bytes accessed | tf_op | source)
XLA Modules:
  0.0 128.2 jit_solution(1021426796558337570)
XLA Ops:
  0.0 0.7 convert_bitcast_fusion.1
  0.7 0.7 convert_bitcast_fusion
  1.4 0.6 pad_maximum_fusion.meta_ref
  2.0 124.4 %shard_map.46 = bf16[128,1536]{1,0:T(8,128)(2,1)} custom-call(bf16[128,3584]{1,0:T(8,128)(2,1)} %tok_ref.1, f32[16,128]{1,0:T(8,128)} %pad_maximum_fusion.meta_ref, bf16[3584,1536]{1,0:T(8,128)(2,1)} %bitcast.5), custom_call_target="tpu_custom_call" | custom-call | flops 11274289152 | bytes 11010048 | tf_op jit(solution)/shard_map/pallas_call | solution.py:392
  126.4 1.8 %copy.6 = bf16[128,1536]{1,0:T(8,128)(2,1)} copy(bf16[128,1536]{1,0:T(8,128)(2,1)} %shard_map.46) | data formatting | bytes 786432

commit v4 on v3

--- a/solution.py
+++ b/solution.py
@@ -380,7 +380,7 @@
     L = lax.axis_size("local")
     cap = T * picks // (G * L)
     FF = w_expert.shape[2]
-    W, WF = tile_of(D, 256), tile_of(FF, 512)
+    W, WF = tile_of(D, 256), tile_of(FF, 256)
     C, N, H = D // W, FF // WF, L // 2
     wide = C * WIDE // 14
     some = max(wide, 1)

time: 128 us -> 137 us (1.070)
  Pallas kernels: 124 us -> 133 us
    pallas_call x1, Pallas kernels: 124 us -> 133 us  [everywhere(): pl.pallas_call(functools.partial(fused_kernel, G, L, cap, W, WF, wide), o...]
where the time goes in v4:
time: 137 us
  Pallas kernels  133 us (97%)
  other arithmetic  1.97 us (1%)
  local copies, waits for them, and re-layouts  1.77 us (1%)
    pallas_call x1, Pallas kernels, everywhere(): pl.pallas_call(functools.partial(fused_kernel, G, L, cap, W, WF, wide), o...  133 us

profile of v4, /device:TPU:0, one launch (start us, length us, event | category | flops | bytes accessed | tf_op | source)
XLA Modules:
  0.0 136.6 jit_solution(6716211777200034648)
XLA Ops:
  0.0 0.7 convert_bitcast_fusion.1
  0.7 0.7 convert_bitcast_fusion
  1.4 0.6 pad_maximum_fusion.meta_ref
  2.0 132.8 %shard_map.46 = bf16[128,1536]{1,0:T(8,128)(2,1)} custom-call(bf16[128,3584]{1,0:T(8,128)(2,1)} %tok_ref.1, f32[16,128]{1,0:T(8,128)} %pad_maximum_fusion.meta_ref, bf16[3584,1536]{1,0:T(8,128)(2,1)} %bitcast.5), custom_call_target="tpu_custom_call" | custom-call | flops 11274289152 | bytes 11010048 | tf_op jit(solution)/shard_map/pallas_call | solution.py:392
  134.8 1.8 %copy.6 = bf16[128,1536]{1,0:T(8,128)(2,1)} copy(bf16[128,1536]{1,0:T(8,128)(2,1)} %shard_map.46) | data formatting | bytes 786432
